TPU v7x, 32 devices: a whole 2x2x4 slice. The times are simulated.
32 devices in a mesh: rows: 8 (over z, x), mem: 4 (over y, core).
Axes of the slice: x: 2, y: 2, z: 4, core: 2. Of those that a mesh axis runs over, the one named last changes fastest.
Arguments:
- factor_panel: float32 [8, 8, 128, 2048], P(None, 'rows'), may hold values from -0.125 to 0.125
- right_side: float32 [8, 8, 128, 128], P(None, 'rows', None, 'mem'), may hold values from -6 to 6
- inverses: float32 [4, 512, 512], replicated, may hold values from -0.125 to 1.5, as said below
Outputs:
- solved: float32 [2048, 128], P(None, 'mem')
- remainder: float32 [8, 8, 128, 128], P(None, 'rows', None, 'mem')
- spread: float32 [8, 8, 128], P(None, 'rows')
Inputs may be any that keep to these rules, and one draw needn't show every extreme that they name: `inverses`: each block is lower triangular with its diagonal between 0.5 and 1.5 and its entries below the diagonal between -0.125 and 0.125.
All inputs are finite; a program needn't handle non-finite values.
Results may differ from a plain program's by a relative error of at most 0.0001.
Values sent between devices are 32-bit elements; how exact they have to be, the bound alone decides.
A program may use at most 64 MiB of HBM per device.

v0:
```python
import jax
import jax.numpy as jnp
from jax import lax
from jax.sharding import PartitionSpec as P

highest = lax.Precision.HIGHEST


def solve_block(inverse, residual_piece, first_owner, tiles_step, tile_rows):
    gathered = lax.all_gather(residual_piece, "rows", axis=0, tiled=True)
    window = lax.slice_in_dim(
        gathered, first_owner * tile_rows, (first_owner + tiles_step) * tile_rows, axis=0
    )
    return jnp.dot(inverse, window, precision=highest, preferred_element_type=jnp.float32)


def shards(factor_panel, right_side, inverses):
    row_devices = lax.axis_size("rows")
    position = lax.axis_index("rows")
    tile_blocks, tile_rows, columns = (
        factor_panel.shape[0],
        factor_panel.shape[2],
        factor_panel.shape[3],
    )
    member_cols = right_side.shape[3]
    lower_rows = factor_panel.reshape(tile_blocks, tile_rows, columns)
    right_rows = right_side.reshape(tile_blocks, tile_rows, member_cols)
    section_count, step_width = (inverses.shape[0], inverses.shape[1])
    tiles_step = step_width // tile_rows
    head_count = min(tile_blocks, -(-(columns // tile_rows) // row_devices))
    global_block = jnp.arange(head_count, dtype=jnp.int32) * row_devices + position
    cutoff = jnp.where(
        global_block * tile_rows < columns, global_block // tiles_step * step_width, columns
    )
    column_ids = jnp.arange(columns, dtype=jnp.int32)
    keep_mask = column_ids[None, None, :] < cutoff[:, None, None]
    masked_head = jnp.where(keep_mask, lower_rows[:head_count], jnp.float32(0.0))
    tail_panel = lower_rows[head_count:]
    blocks = []
    for section in range(section_count):
        first_tile = section * tiles_step
        block_slot = first_tile // row_devices
        first_owner = first_tile % row_devices
        start = section * step_width
        residual_piece = right_rows[block_slot]
        if section > 0:
            earlier = jnp.concatenate(blocks, axis=0)
            residual_piece = residual_piece - jnp.dot(
                masked_head[block_slot][:, :start],
                earlier,
                precision=highest,
                preferred_element_type=jnp.float32,
            )
        blocks.append(
            solve_block(inverses[section], residual_piece, first_owner, tiles_step, tile_rows)
        )
    solved = jnp.concatenate(blocks, axis=0)
    head_left = right_rows[:head_count] - jnp.einsum(
        "jrc,cm->jrm", masked_head, solved, precision=highest, preferred_element_type=jnp.float32
    )
    tail_left = right_rows[head_count:] - jnp.einsum(
        "jrc,cm->jrm", tail_panel, solved, precision=highest, preferred_element_type=jnp.float32
    )
    remainder = jnp.concatenate([head_left, tail_left], axis=0)
    member_total = jnp.sum(remainder, axis=2)
    squares = jnp.sum(remainder * remainder, axis=2)
    member_total, squares = lax.psum((member_total, squares), "mem")
    member_count = member_cols * lax.axis_size("mem")
    member_mean = member_total / member_count
    spread = squares / member_count - member_mean * member_mean
    return (solved, remainder.reshape(right_side.shape), spread.reshape(tile_blocks, 1, tile_rows))


def solution(mesh):
    return jax.shard_map(
        shards,
        mesh=mesh,
        in_specs=(P(None, "rows", None, None), P(None, "rows", None, "mem"), P()),
        out_specs=(P(None, "mem"), P(None, "rows", None, "mem"), P(None, "rows", None)),
        check_vma=False,
    )
```

profile of v0, /device:TPU:0, one launch (start us, length us, event | category | flops | bytes accessed | tf_op | source)
XLA Modules:
  0.0 149.8 jit_solution(8177884290052563035)
XLA Ops:
  0.7 0.1 iota_compare_fusion
  0.7 0.7 slice.75
  1.5 32.3 %all-gather = f32[1,1,1024,32]{2,3,1,0:T(8,128)S(1)} all-gather(f32[1,1,128,32]{2,3,1,0:T(8,128)S(1)} %slice.75), channel_id=2, replica_groups=mesh['rows'=8,'mem'=4] {'rows'}, dimensions={2}, use_global_device_ids=true | all-gather | bytes 147456 | tf_op jit(solution)/shard_map/all_gather | solution.py:10
  33.8 0.0 copy-start.2
  33.8 2.3 %fusion.6 = f32[512,32]{0,1:T(8,128)S(1)} fusion(f32[4,512,512]{2,1,0:T(8,128)} %param.5, f32[1,1,1024,32]{2,3,1,0:T(8,128)S(1)} %all-gather), kind=kOutput, calls=%fused_computation.17 | convolution fusion | flops 100663296 | bytes 1179648 | tf_op jit(solution)/shard_map/dot_general | solution.py:14
  36.1 0.0 copy-start
  36.1 0.0 slice-start
  36.1 2.0 %bitcast_select_fusion = f32[2,128,2048]{2,1,0:T(8,128)S(1)} fusion(f32[8,1,128,2048]{3,2,1,0:T(8,128)} %param.3, pred[2,2048]{1,0:T(4,128)(4,1)S(1)} %iota_compare_fusion), kind=kLoop, calls=%fused_computation.2 | loop fusion | flops 524288 | bytes 4198400 | tf_op jit(solution)/shard_map/jit(_where)/select_n | solution.py:37
  38.1 0.2 slice_bitcast_fusion.7
  38.3 0.0 copy-done.2
  38.3 0.0 slice-start.1
  38.3 0.4 convolution_subtract_fusion.3
  38.6 30.7 %all_gather.13 = f32[1024,32]{0,1:T(8,128)S(1)} all-gather(f32[128,32]{0,1:T(8,128)S(1)} %convolution_subtract_fusion.3), channel_id=1, replica_groups=mesh['rows'=8,'mem'=4] {'rows'}, dimensions={0}, use_global_device_ids=true | all-gather | bytes 147456 | tf_op jit(solution)/shard_map/all_gather | solution.py:10
  69.3 0.0 copy-done
  69.3 1.0 convolution_bitcast_fusion.2
  70.4 0.6 convolution_subtract_fusion.2
  71.0 30.5 %all_gather.14 = f32[1024,32]{0,1:T(8,128)S(1)} all-gather(f32[128,32]{0,1:T(8,128)S(1)} %convolution_subtract_fusion.2), channel_id=1, replica_groups=mesh['rows'=8,'mem'=4] {'rows'}, dimensions={0}, use_global_device_ids=true | all-gather | bytes 147456 | tf_op jit(solution)/shard_map/all_gather | solution.py:10
  101.5 1.0 convolution_bitcast_fusion.1
  102.6 0.8 convolution_subtract_fusion.1
  103.4 30.5 %all_gather.15 = f32[1024,32]{0,1:T(8,128)S(1)} all-gather(f32[128,32]{0,1:T(8,128)S(1)} %convolution_subtract_fusion.1), channel_id=1, replica_groups=mesh['rows'=8,'mem'=4] {'rows'}, dimensions={0}, use_global_device_ids=true | all-gather | bytes 147456 | tf_op jit(solution)/shard_map/all_gather | solution.py:10
  133.9 1.0 convolution_bitcast_fusion
  135.0 0.0 copy-start.1
  135.0 1.9 %convolution_subtract_fusion = f32[2,128,32]{1,2,0:T(8,128)S(1)} fusion(f32[2,128,2048]{2,1,0:T(8,128)S(1)} %bitcast_select_fusion, f32[2048,32]{0,1:T(8,128)S(1)} %pad_maximum_fusion, f32[8,1,128,32]{2,3,0,1:T(8,128)S(1)} %bitcast.69), kind=kOutput, calls=%fused_computation.8 | convolution fusion | flops 201334784 | bytes 2424832 | tf_op jit(solution)/shard_map/jrc,cm->jrm/dot_general | solution.py:58
  136.9 0.0 slice-done
  136.9 0.0 slice-done.1
  136.9 5.8 %fusion.2 = f32[6,128,32]{1,2,0:T(8,128)S(1)} fusion(f32[8,1,128,2048]{3,2,0,1:T(8,128)S(1)} %bitcast.68, f32[2048,32]{0,1:T(8,128)S(1)} %pad_maximum_fusion, f32[8,1,128,32]{2,3,0,1:T(8,128)S(1)} %bitcast.70), kind=kOutput, calls=%fused_computation.4 | convolution fusion | flops 604004352 | bytes 6750208 | tf_op jit(solution)/shard_map/jrc,cm->jrm/dot_general | solution.py:61
  142.7 0.0 copy-done.1
  142.7 0.7 multiply_reduce_fusion
  143.4 5.7 %all-reduce = (f32[8,128]{1,0:T(8,128)S(1)}, f32[8,128]{1,0:T(8,128)S(1)}) all-reduce(f32[8,128]{1,0:T(8,128)S(1)} %get-tuple-element.7, f32[8,128]{1,0:T(8,128)S(1)} %get-tuple-element.6), channel_id=1, replica_groups=mesh['rows'=8,'mem'=4] {'mem'}, use_global_device_ids=true, to_apply=%region_3.4 | all-reduce | flops 2048 | bytes 16384 | tf_op jit(solution)/shard_map/psum | solution.py:67
  149.2 0.6 multiply_subtract_fusion
  (3 shorter events, 0.0 us)
Async XLA Ops:
  33.8 4.5 %copy-start.2 = (f32[8,1,128,32]{2,3,1,0:T(8,128)S(1)}, f32[8,1,128,32]{2,3,1,0:T(8,128)}, u32[]{:S(2)}) copy-start(f32[8,1,128,32]{2,3,1,0:T(8,128)} %param.4) | copy-start | bytes 393220
  36.1 33.2 %copy-start = (f32[4,512,512]{2,1,0:T(8,128)S(1)}, f32[4,512,512]{2,1,0:T(8,128)}, u32[]{:S(2)}) copy-start(f32[4,512,512]{2,1,0:T(8,128)} %param.5) | copy-start | bytes 12582916
  36.1 100.8 %slice-start = ((s8[8388608]{0:T(1024)(128)(4,1)}), s8[4194304]{0:T(1024)(128)(4,1)S(1)}, s32[]{:S(2)}) async-start(s8[8388608]{0:T(1024)(128)(4,1)} %bitcast.66), calls=%async_computation | async-start | bytes 8388608
  38.3 98.7 %slice-start.1 = ((s8[8388608]{0:T(1024)(128)(4,1)}), s8[4194304]{0:T(1024)(128)(4,1)S(1)}, s32[]{:S(2)}) async-start(s8[8388608]{0:T(1024)(128)(4,1)} %bitcast.66), calls=%async_computation.1 | async-start | bytes 8388608
  135.0 7.7 %copy-start.1 = (f32[2048,32]{0,1:T(8,128)}, f32[2048,32]{0,1:T(8,128)S(1)}, u32[]{:S(2)}) copy-start(f32[2048,32]{0,1:T(8,128)S(1)} %pad_maximum_fusion) | copy-start | bytes 786436
where the time goes:
time: 150 us
  blocking collectives  130 us (87%)
  matrix products  14.9 us (10%)
  other arithmetic  3.34 us (2%)
    all_gather x4, blocking collectives, solve_block(): gathered = lax.all_gather(residual_piece, 'rows', axis=0, tiled=True)  124 us
    dot_general x1, matrix products, shards(): jnp.einsum('jrc,cm->jrm', tail_panel, solved, precision=highest, preferre...  5.78 us
    psum x1, blocking collectives, shards(): member_total, squares = lax.psum((member_total, squares), 'mem')  5.74 us
    dot_general x4, matrix products, solve_block(): jnp.dot(inverse, window, precision=highest, preferred_element_type=jnp.fl...  5.46 us

commit v1 on v0

v1 whole, which is shorter than its diff:
```python
import functools

import jax
import jax.numpy as jnp
from jax import lax
from jax.experimental import pallas as pl
from jax.experimental.pallas import tpu as pltpu
from jax.sharding import PartitionSpec as P

f32 = jnp.float32
bf16 = jnp.bfloat16
MESH = pl.DeviceIdType.MESH


def split(x):
    high = x.astype(bf16)
    return high, (x - high.astype(f32)).astype(bf16)


def dot_nt(a, b):
    return lax.dot_general(a, b, (((1,), (1,)), ((), ())), preferred_element_type=f32)


def dot_nn(a, b):
    return lax.dot_general(a, b, (((1,), (0,)), ((), ())), preferred_element_type=f32)


def product(stacked, weight_high, weight_low, dot=dot_nt):
    half = stacked.shape[0] // 2
    both = dot(stacked, weight_high)
    return both[:half] + both[half:] + dot(stacked[:half], weight_low)


def stack(x):
    return jnp.concatenate(split(x), axis=0)


def kernel(
    row_devices,
    mem_devices,
    panel_hbm,
    right_hbm,
    inverse_hbm,
    solved,
    left,
    spread_ref,
    panel,
    inverse,
    pieces,
    gain_high,
    gain_low,
    sums,
    panel_sem,
    inverse_sem,
    right_sem,
    send_sem,
    recv_sem,
    sums_send_sem,
    sums_recv_sem,
):
    p = lax.axis_index("rows")
    m = lax.axis_index("mem")
    steps, tile_blocks, tile, width = panel.shape
    tiles = width // tile
    heads = min(tile_blocks, -(-(steps * tiles) // row_devices))
    members = left.shape[1]

    load_right = pltpu.make_async_copy(right_hbm, left, right_sem)
    load_right.start()
    load_panel, load_inverse = [], []
    for s in range(steps):
        load_inverse.append(
            pltpu.make_async_copy(inverse_hbm.at[s], inverse.at[s], inverse_sem.at[s])
        )
        load_inverse[s].start()
        load_panel.append(
            pltpu.make_async_copy(
                panel_hbm.at[:, :, pl.ds(s * width, width)], panel.at[s], panel_sem.at[s]
            )
        )
        load_panel[s].start()

    barrier = pltpu.get_barrier_semaphore()
    for k in range(1, row_devices):
        pl.semaphore_signal(
            barrier, inc=1, device_id=(lax.rem(p + k, row_devices), m), device_id_type=MESH
        )
    for k in range(1, mem_devices):
        pl.semaphore_signal(
            barrier, inc=1, device_id=(p, lax.rem(m + k, mem_devices)), device_id_type=MESH
        )
    load_right.wait()
    pl.semaphore_wait(barrier, row_devices + mem_devices - 2)

    def owner(s):
        place = p - (s * tiles) % row_devices
        return place, jnp.logical_and(place >= 0, place < tiles)

    def slot_of(s):
        return (s * tiles) // row_devices

    def copy_to(s, place, k):
        target = ((s + 1) * tiles + k) % row_devices
        return target, pltpu.make_async_remote_copy(
            src_ref=pieces.at[s, place],
            dst_ref=pieces.at[s, place],
            send_sem=send_sem.at[s, k],
            recv_sem=recv_sem.at[s, place],
            device_id=(target, m),
            device_id_type=MESH,
        )

    def send(s, residual):
        place, _ = owner(s)
        pieces[s, place] = residual
        for k in range(row_devices):
            target, copy = copy_to(s, place, k)

            @pl.when(target != p)
            def _():
                copy.start()

    def receive(s):
        for i in range(tiles):
            source = (s * tiles) % row_devices + i

            @pl.when(source != p)
            def _():
                pltpu.make_async_remote_copy(
                    src_ref=pieces.at[s, i],
                    dst_ref=pieces.at[s, i],
                    send_sem=send_sem.at[s, 0],
                    recv_sem=recv_sem.at[s, i],
                    device_id=(source, m),
                    device_id_type=MESH,
                ).wait_recv()

        return stack(jnp.concatenate([pieces[s, i] for i in range(tiles)], axis=1))

    def make_gain(s):
        load_inverse[s].wait()
        load_panel[s].wait()
        if s + 1 < steps:
            _, mine = owner(s + 1)

            @pl.when(mine)
            def _():
                high, low = split(inverse[s])
                gain = product(stack(panel[s, slot_of(s + 1)]), high, low, dot_nn)
                gain_high[s], gain_low[s] = split(gain)

    _, first = owner(0)

    @pl.when(first)
    def _():
        send(0, left[slot_of(0)])

    for s in range(steps):
        make_gain(s)
        residual = receive(s)
        if s + 1 < steps:
            _, mine = owner(s + 1)

            @pl.when(mine)
            def _():
                slot = slot_of(s + 1)
                new = left[slot] - product(residual, gain_high[s], gain_low[s])
                left[slot] = new
                send(s + 1, new)

        high, low = split(inverse[s])
        block = product(residual, high, low)
        solved[:, s * width : (s + 1) * width] = block
        block = stack(block)
        for j in range(heads):
            level = (j * row_devices + p) // tiles
            due = level > s + 1 if s + 1 < steps else level >= steps

            @pl.when(due)
            def _():
                high, low = split(panel[s, j])
                left[j] = left[j] - product(block, high, low)

        for j in range(heads, tile_blocks, 2):
            count = min(2, tile_blocks - j)
            high, low = split(panel[s, j : j + count].reshape(count * tile, width))
            change = product(block, high, low)
            for i in range(count):
                left[j + i] = left[j + i] - change[:, i * tile : (i + 1) * tile]

    value = left[...]
    sums[m] = jnp.stack([jnp.sum(value, axis=1), jnp.sum(value * value, axis=1)])

    def sums_copy(k):
        return pltpu.make_async_remote_copy(
            src_ref=sums.at[m],
            dst_ref=sums.at[m],
            send_sem=sums_send_sem.at[k],
            recv_sem=sums_recv_sem.at[m],
            device_id=(p, lax.rem(m + k, mem_devices)),
            device_id_type=MESH,
        )

    for k in range(1, mem_devices):
        sums_copy(k).start()
    for s in range(steps):
        place, mine = owner(s)

        @pl.when(mine)
        def _():
            for k in range(row_devices):
                target, copy = copy_to(s, place, k)

                @pl.when(target != p)
                def _():
                    copy.wait_send()

    for k in range(1, mem_devices):
        other = lax.rem(m + k, mem_devices)
        pltpu.make_async_remote_copy(
            src_ref=sums.at[other],
            dst_ref=sums.at[other],
            send_sem=sums_send_sem.at[k],
            recv_sem=sums_recv_sem.at[other],
            device_id=(p, other),
            device_id_type=MESH,
        ).wait_recv()
    total = sums[0]
    for k in range(1, mem_devices):
        total = total + sums[k]
    mean = total / (members * mem_devices)
    spread_ref[...] = mean[1] - mean[0] * mean[0]
    for k in range(1, mem_devices):
        sums_copy(k).wait_send()


def shards(row_devices, mem_devices, factor_panel, right_side, inverses):
    tile_blocks, _, tile, columns = factor_panel.shape
    members = right_side.shape[3]
    steps, width, _ = inverses.shape
    tiles = width // tile
    panel = factor_panel.reshape(tile_blocks, tile, columns)
    right = jnp.swapaxes(right_side.reshape(tile_blocks, tile, members), 1, 2)
    hbm = pl.BlockSpec(memory_space=pltpu.HBM)
    vmem = pl.BlockSpec(memory_space=pltpu.VMEM)
    dma = pltpu.SemaphoreType.DMA
    solved, remainder, spread = pl.pallas_call(
        functools.partial(kernel, row_devices, mem_devices),
        out_shape=(
            jax.ShapeDtypeStruct((members, columns), f32),
            jax.ShapeDtypeStruct((tile_blocks, members, tile), f32),
            jax.ShapeDtypeStruct((tile_blocks, tile), f32),
        ),
        in_specs=[hbm] * 3,
        out_specs=(vmem, vmem, vmem),
        scratch_shapes=[
            pltpu.VMEM((steps, tile_blocks, tile, width), f32),
            pltpu.VMEM((steps, width, width), f32),
            pltpu.VMEM((steps, tiles, members, tile), f32),
            pltpu.VMEM((steps, tile, width), bf16),
            pltpu.VMEM((steps, tile, width), bf16),
            pltpu.VMEM((mem_devices, 2, tile_blocks, tile), f32),
            dma((steps,)),
            dma((steps,)),
            dma,
            dma((steps, row_devices)),
            dma((steps, tiles)),
            dma((mem_devices,)),
            dma((mem_devices,)),
        ],
        compiler_params=pltpu.CompilerParams(
            collective_id=0, has_side_effects=True, vmem_limit_bytes=48 * 1024 * 1024
        ),
    )(panel, right, inverses)
    return (
        solved.T,
        jnp.swapaxes(remainder, 1, 2).reshape(right_side.shape),
        spread.reshape(tile_blocks, 1, tile),
    )


def solution(mesh):
    return jax.shard_map(
        functools.partial(shards, mesh.shape["rows"], mesh.shape["mem"]),
        mesh=mesh,
        in_specs=(P(None, "rows", None, None), P(None, "rows", None, "mem"), P()),
        out_specs=(P(None, "mem"), P(None, "rows", None, "mem"), P(None, "rows", None)),
        check_vma=False,
    )
```

time: 150 us -> 35.8 us (0.24)
  blocking collectives: 130 us -> 0 us
  Pallas kernels: 0 us -> 30 us
  matrix products: 14.9 us -> 0 us
  local copies, waits for them, and re-layouts: 0.93 us -> 5.04 us
  other arithmetic: 3.34 us -> 0 us
    all_gather x4 -> x0, blocking collectives: 124 us -> none  [solve_block(): gathered = lax.all_gather(residual_piece, 'rows', axis=0, tiled=True)]
    pallas_call x0 -> x1, Pallas kernels: none -> 30 us  [shards(): pl.pallas_call(functools.partial(kernel, row_devices, mem_devices), out_s...]
    dot_general x9 -> x0, matrix products: 14.9 us -> none  [the longest x1 5.78 us: shards(): jnp.einsum('jrc,cm->jrm', tail_panel, solved, precision=highest, preferre...]
    psum x1 -> x0, blocking collectives: 5.74 us -> none  [shards(): member_total, squares = lax.psum((member_total, squares), 'mem')]
    unnamed x10 -> x7, local copies, waits for them, and re-layouts: 0.03 us -> 5.04 us
    select_n x2 -> x0, other arithmetic: 1.97 us -> none  [the longest x1 1.96 us: shards(): jnp.where(keep_mask, lower_rows[:head_count], jnp.float32(0.0))]
where the time goes in v1:
time: 35.8 us; the launch traced here: 35.6 us
  Pallas kernels  30 us (84%)
  local copies, waits for them, and re-layouts  5.04 us (14%)
  between operations  0.65 us (2%)
    pallas_call x1, Pallas kernels, shards(): pl.pallas_call(functools.partial(kernel, row_devices, mem_devices), out_s...  30 us
    unnamed x7, local copies, waits for them, and re-layouts  5.04 us

profile of v1, /device:TPU:0, one launch (start us, length us, event | category | flops | bytes accessed | tf_op | source)
XLA Modules:
  0.0 35.6 jit_solution(2379314680009337803)
XLA Ops:
  0.6 0.0 copy-start
  0.6 2.2 %copy-done = f32[4,512,512]{2,1,0:T(8,128)S(1)} copy-done((f32[4,512,512]{2,1,0:T(8,128)S(1)}, f32[4,512,512]{2,1,0:T(8,128)}, u32[]{:S(2)}) %copy-start) | copy-done | bytes 4194328
  2.8 0.0 copy-start.1
  2.8 0.9 %copy-done.1 = f32[8,1,128,32]{2,3,1,0:T(8,128)S(1)} copy-done((f32[8,1,128,32]{2,3,1,0:T(8,128)S(1)}, f32[8,1,128,32]{2,3,1,0:T(8,128)}, u32[]{:S(2)}) %copy-start.1) | copy-done | bytes 131096
  3.7 30.0 %shard_map.58 = (f32[32,2048]{1,0:T(8,128)S(1)}, f32[8,32,128]{2,1,0:T(8,128)S(1)}, f32[8,128]{1,0:T(8,128)S(1)}) custom-call(f32[8,128,2048]{2,1,0:T(8,128)} %bitcast.17, f32[8,32,128]{2,1,0:T(8,128)S(1)} %bitcast.14, f32[4,512,512]{2,1,0:T(8,128)S(1)} %copy-done), custom_call_target="tpu_custom_call" | custom-call | tf_op jit(solution)/shard_map/pallas_call | solution.py:247
  33.7 0.7 %copy.11 = f32[2048,32]{0,1:T(8,128)} copy(f32[2048,32]{0,1:T(8,128)S(1)} %bitcast.13) | data formatting | bytes 524288
  34.4 0.7 %copy.12 = f32[8,1,128,32]{2,3,1,0:T(8,128)} copy(f32[8,1,128,32]{2,3,1,0:T(8,128)S(1)} %bitcast.15) | data formatting | bytes 262144
  35.0 0.6 %copy.13 = f32[8,1,128]{2,1,0:T(1,128)} copy(f32[8,1,128]{2,1,0:T(1,128)S(1)} %bitcast.16) | data formatting | bytes 8192
Async XLA Ops:
  0.6 2.2 %copy-start = (f32[4,512,512]{2,1,0:T(8,128)S(1)}, f32[4,512,512]{2,1,0:T(8,128)}, u32[]{:S(2)}) copy-start(f32[4,512,512]{2,1,0:T(8,128)} %inverse_hbm.1) | copy-start | bytes 12582916
  2.8 0.9 %copy-start.1 = (f32[8,1,128,32]{2,3,1,0:T(8,128)S(1)}, f32[8,1,128,32]{2,3,1,0:T(8,128)}, u32[]{:S(2)}) copy-start(f32[8,1,128,32]{2,3,1,0:T(8,128)} %param.4) | copy-start | bytes 393220

commit v2 on v1

--- a/solution.py
+++ b/solution.py
@@ -232,6 +232,29 @@
     spread_ref[...] = mean[1] - mean[0] * mean[0]
     for k in range(1, mem_devices):
         sums_copy(k).wait_send()
+
+
+def store_kernel(*refs):
+    count = (len(refs) - 1) // 2
+    copies = [
+        pltpu.make_async_copy(refs[i], refs[count + i], refs[-1].at[i]) for i in range(count)
+    ]
+    for copy in copies:
+        copy.start()
+    for copy in copies:
+        copy.wait()
+
+
+def store(*arrays):
+    spec = pl.BlockSpec(memory_space=pl.ANY)
+    return pl.pallas_call(
+        store_kernel,
+        out_shape=tuple(jax.ShapeDtypeStruct(a.shape, a.dtype) for a in arrays),
+        in_specs=[spec] * len(arrays),
+        out_specs=(spec,) * len(arrays),
+        scratch_shapes=[pltpu.SemaphoreType.DMA((len(arrays),))],
+        compiler_params=pltpu.CompilerParams(vmem_limit_bytes=1024 * 1024),
+    )(*arrays)
 
 
 def shards(row_devices, mem_devices, factor_panel, right_side, inverses):
@@ -269,9 +292,10 @@
             dma((mem_devices,)),
         ],
         compiler_params=pltpu.CompilerParams(
-            collective_id=0, has_side_effects=True, vmem_limit_bytes=48 * 1024 * 1024
+            collective_id=0, has_side_effects=True, vmem_limit_bytes=52 * 1024 * 1024
         ),
     )(panel, right, inverses)
+    solved, remainder, spread = store(solved, remainder, spread)
     return (
         solved.T,
         jnp.swapaxes(remainder, 1, 2).reshape(right_side.shape),

time: 35.8 us -> 32.1 us (0.90)
  local copies, waits for them, and re-layouts: 5.04 us -> 0.9 us
  Pallas kernels: 30 us -> 30.4 us
    unnamed x7 -> x2, local copies, waits for them, and re-layouts: 5.04 us -> 0.9 us
    pallas_call x0 -> x1, Pallas kernels: none -> 0.77 us  [store(): pl.pallas_call(store_kernel, out_shape=tuple((jax.ShapeDtypeStruct(a.shap...]
where the time goes in v2:
time: 32.1 us; the launch traced here: 32 us
  Pallas kernels  30.4 us (95%)
  local copies, waits for them, and re-layouts  0.9 us (3%)
  between operations  0.65 us (2%)
    pallas_call x1, Pallas kernels, shards(): pl.pallas_call(functools.partial(kernel, row_devices, mem_devices), out_s...  29.7 us
    unnamed x2, local copies, waits for them, and re-layouts  0.9 us
    pallas_call x1, Pallas kernels, store(): pl.pallas_call(store_kernel, out_shape=tuple((jax.ShapeDtypeStruct(a.shap...  0.77 us

profile of v2, /device:TPU:0, one launch (start us, length us, event | category | flops | bytes accessed | tf_op | source)
XLA Modules:
  0.0 32.0 jit_solution(3288870149462856352)
XLA Ops:
  0.6 0.0 copy-start
  0.6 0.9 %copy-done = f32[8,1,128,32]{2,3,1,0:T(8,128)S(1)} copy-done((f32[8,1,128,32]{2,3,1,0:T(8,128)S(1)}, f32[8,1,128,32]{2,3,1,0:T(8,128)}, u32[]{:S(2)}) %copy-start) | copy-done | bytes 131096
  1.5 29.7 %shard_map.58 = (f32[32,2048]{1,0:T(8,128)S(1)}, f32[8,32,128]{2,1,0:T(8,128)S(1)}, f32[8,128]{1,0:T(8,128)S(1)}) custom-call(f32[8,128,2048]{2,1,0:T(8,128)} %bitcast.14, f32[8,32,128]{2,1,0:T(8,128)S(1)} %bitcast.13, f32[4,512,512]{2,1,0:T(8,128)} %inverse_hbm.1), custom_call_target="tpu_custom_call" | custom-call | tf_op jit(solution)/shard_map/pallas_call | solution.py:270
  31.2 0.8 %shard_map.59 = (f32[32,2048]{1,0:T(8,128)}, f32[8,32,128]{2,1,0:T(8,128)}, f32[8,128]{1,0:T(8,128)}) custom-call(f32[32,2048]{1,0:T(8,128)S(1)} %get-tuple-element.9.refs_0_, f32[8,32,128]{2,1,0:T(8,128)S(1)} %get-tuple-element.10.refs_1_, f32[8,128]{1,0:T(8,128)S(1)} %get-tuple-element.11.refs_2_), custom_call_target="tpu_custom_call" | custom-call | tf_op jit(solution)/shard_map/pallas_call | solution.py:250
Async XLA Ops:
  0.6 0.9 %copy-start = (f32[8,1,128,32]{2,3,1,0:T(8,128)S(1)}, f32[8,1,128,32]{2,3,1,0:T(8,128)}, u32[]{:S(2)}) copy-start(f32[8,1,128,32]{2,3,1,0:T(8,128)} %param.4) | copy-start | bytes 393220

commit v3 on v2

--- a/solution.py
+++ b/solution.py
@@ -49,6 +49,8 @@
     pieces,
     gain_high,
     gain_low,
+    last_high,
+    last_low,
     sums,
     panel_sem,
     inverse_sem,
@@ -149,14 +151,41 @@
                 gain = product(stack(panel[s, slot_of(s + 1)]), high, low, dot_nn)
                 gain_high[s], gain_low[s] = split(gain)
 
+    def slot_groups():
+        groups = [
+            (j, 1, (j * row_devices + p) // tiles >= steps) for j in range(heads)
+        ]
+        for j in range(heads, tile_blocks, 2):
+            groups.append((j, min(2, tile_blocks - j), True))
+        return groups
+
+    def make_last():
+        high, low = split(inverse[steps - 1])
+        for j, count, due in slot_groups():
+
+            @pl.when(due)
+            def _():
+                rows = panel[steps - 1, j : j + count].reshape(count * tile, width)
+                gain = split(product(stack(rows), high, low, dot_nn))
+                last_high[j * tile : (j + count) * tile] = gain[0]
+                last_low[j * tile : (j + count) * tile] = gain[1]
+
     _, first = owner(0)
 
     @pl.when(first)
     def _():
         send(0, left[slot_of(0)])
 
+    def solve(s, residual):
+        high, low = split(inverse[s])
+        block = product(residual, high, low)
+        solved[:, s * width : (s + 1) * width] = block
+        return stack(block)
+
     for s in range(steps):
         make_gain(s)
+        if s == steps - 1:
+            make_last()
         residual = receive(s)
         if s + 1 < steps:
             _, mine = owner(s + 1)
@@ -168,15 +197,13 @@
                 left[slot] = new
                 send(s + 1, new)
 
-        high, low = split(inverse[s])
-        block = product(residual, high, low)
-        solved[:, s * width : (s + 1) * width] = block
-        block = stack(block)
+        if s == steps - 1:
+            break
+        block = solve(s, residual)
         for j in range(heads):
             level = (j * row_devices + p) // tiles
-            due = level > s + 1 if s + 1 < steps else level >= steps
-
-            @pl.when(due)
+
+            @pl.when(level > s + 1)
             def _():
                 high, low = split(panel[s, j])
                 left[j] = left[j] - product(block, high, low)
@@ -185,6 +212,15 @@
             count = min(2, tile_blocks - j)
             high, low = split(panel[s, j : j + count].reshape(count * tile, width))
             change = product(block, high, low)
+            for i in range(count):
+                left[j + i] = left[j + i] - change[:, i * tile : (i + 1) * tile]
+
+    for j, count, due in slot_groups():
+
+        @pl.when(due)
+        def _():
+            rows = pl.ds(j * tile, count * tile)
+            change = product(residual, last_high[rows], last_low[rows])
             for i in range(count):
                 left[j + i] = left[j + i] - change[:, i * tile : (i + 1) * tile]
 
@@ -203,6 +239,7 @@
 
     for k in range(1, mem_devices):
         sums_copy(k).start()
+    solve(steps - 1, residual)
     for s in range(steps):
         place, mine = owner(s)
 
@@ -282,6 +319,8 @@
             pltpu.VMEM((steps, tiles, members, tile), f32),
             pltpu.VMEM((steps, tile, width), bf16),
             pltpu.VMEM((steps, tile, width), bf16),
+            pltpu.VMEM((tile_blocks * tile, width), bf16),
+            pltpu.VMEM((tile_blocks * tile, width), bf16),
             pltpu.VMEM((mem_devices, 2, tile_blocks, tile), f32),
             dma((steps,)),
             dma((steps,)),

time: 32.1 us -> 31.7 us (0.988)
  Pallas kernels: 30.4 us -> 30 us
    pallas_call x1, Pallas kernels: 29.7 us -> 29.2 us  [shards(): pl.pallas_call(functools.partial(kernel, row_devices, mem_devices), out_s...]
where the time goes in v3:
time: 31.7 us; the launch traced here: 31.5 us
  Pallas kernels  30 us (95%)
  local copies, waits for them, and re-layouts  0.9 us (3%)
  between operations  0.65 us (2%)
    pallas_call x1, Pallas kernels, shards(): pl.pallas_call(functools.partial(kernel, row_devices, mem_devices), out_s...  29.2 us
    unnamed x2, local copies, waits for them, and re-layouts  0.9 us
    pallas_call x1, Pallas kernels, store(): pl.pallas_call(store_kernel, out_shape=tuple((jax.ShapeDtypeStruct(a.shap...  0.77 us

profile of v3, /device:TPU:0, one launch (start us, length us, event | category | flops | bytes accessed | tf_op | source)
XLA Modules:
  0.0 31.5 jit_solution(10789824650565226738)
XLA Ops:
  0.6 0.0 copy-start
  0.6 0.9 %copy-done = f32[8,1,128,32]{2,3,1,0:T(8,128)S(1)} copy-done((f32[8,1,128,32]{2,3,1,0:T(8,128)S(1)}, f32[8,1,128,32]{2,3,1,0:T(8,128)}, u32[]{:S(2)}) %copy-start) | copy-done | bytes 131096
  1.5 29.2 %shard_map.58 = (f32[32,2048]{1,0:T(8,128)S(1)}, f32[8,32,128]{2,1,0:T(8,128)S(1)}, f32[8,128]{1,0:T(8,128)S(1)}) custom-call(f32[8,128,2048]{2,1,0:T(8,128)} %bitcast.14, f32[8,32,128]{2,1,0:T(8,128)S(1)} %bitcast.13, f32[4,512,512]{2,1,0:T(8,128)} %inverse_hbm.1), custom_call_target="tpu_custom_call" | custom-call | tf_op jit(solution)/shard_map/pallas_call | solution.py:307
  30.8 0.8 %shard_map.59 = (f32[32,2048]{1,0:T(8,128)}, f32[8,32,128]{2,1,0:T(8,128)}, f32[8,128]{1,0:T(8,128)}) custom-call(f32[32,2048]{1,0:T(8,128)S(1)} %get-tuple-element.9.refs_0_, f32[8,32,128]{2,1,0:T(8,128)S(1)} %get-tuple-element.10.refs_1_, f32[8,128]{1,0:T(8,128)S(1)} %get-tuple-element.11.refs_2_), custom_call_target="tpu_custom_call" | custom-call | tf_op jit(solution)/shard_map/pallas_call | solution.py:287
Async XLA Ops:
  0.6 0.9 %copy-start = (f32[8,1,128,32]{2,3,1,0:T(8,128)S(1)}, f32[8,1,128,32]{2,3,1,0:T(8,128)}, u32[]{:S(2)}) copy-start(f32[8,1,128,32]{2,3,1,0:T(8,128)} %param.4) | copy-start | bytes 393220
